TPU v7x, 512 devices: a whole 4x8x8 slice. The times are simulated.
512 devices in a mesh: group: 16 (over y, z_lo), fsdp: 32 (over z_hi, x, core).
Axes of the slice: x: 4, y: 8, z: 8 (z_hi: 4, z_lo: 2; z = z_hi * 2 + z_lo), core: 2. Of those that a mesh axis runs over, the one named last changes fastest.
Arguments:
- activations: bfloat16 [16, 5120, 5120], P('group', 'fsdp'), may hold values from -6 to 6
- cotangent: bfloat16 [16, 5120, 1024], P('group', 'fsdp'), may hold values from -384 to 384
- live: int32 [16, 32], P('group', 'fsdp'), may hold values from 1 to 160, as said below
- local_params: bfloat16 [16, 5120, 1024], P('group', 'fsdp'), may hold values from -6 to 6
- anchor: float32 [32, 160, 1024], P('fsdp', 'group'), may hold values from -6 to 6
- momentum: float32 [32, 160, 1024], P('fsdp', 'group'), may hold values from -6 to 6
Outputs:
- new_params: bfloat16 [5120, 1024], P('fsdp')
- new_anchor: float32 [32, 160, 1024], P('fsdp', 'group')
- new_momentum: float32 [32, 160, 1024], P('fsdp', 'group')
Inputs may be any that keep to these rules, and one draw needn't show every extreme that they name: Within a group the live counts of its devices are independent; one device of the last group is full.
All inputs are finite; a program needn't handle non-finite values.
Results may differ from a plain program's by a relative error of at most 0.0095.
Values may be sent and summed in bfloat16 or wider, within the bound.
A program may use at most 64 MiB of HBM per device.

v0:
```python
import jax
import jax.numpy as jnp
from jax import lax
from jax.sharding import PartitionSpec as P


def local(activations, cotangent, live, local_params, anchor, momentum):
    groups = lax.axis_size("group")
    group_index = lax.axis_index("group")
    slots = cotangent.shape[1]
    keep = jnp.arange(slots, dtype=jnp.int32) < live[0, 0]
    masked = jnp.where(keep[:, None], cotangent[0], jnp.zeros_like(cotangent[0]))
    selector = jnp.arange(groups, dtype=jnp.int32) == group_index
    own_count = jnp.where(selector, live[0, 0].astype(jnp.float32), 0.0)
    counts_all = lax.psum(own_count, ("group", "fsdp"))
    count = jnp.sum(jnp.where(selector, counts_all, 0.0))
    total = jnp.sum(counts_all)
    columns = lax.all_to_all(activations[0], "fsdp", split_axis=1, concat_axis=0, tiled=True)
    summed = lax.dot_general(
        columns,
        lax.all_gather(masked, "fsdp", axis=0, tiled=True),
        (((0,), (0,)), ((), ())),
        preferred_element_type=jnp.float32,
    )
    inner = local_params[0].astype(jnp.float32) - 0.5 * (summed / count)
    weighted = count / total * inner
    average = lax.psum_scatter(weighted, "group", scatter_dimension=0, tiled=True)
    delta = anchor[0] - average
    moment = 0.9 * momentum[0] + delta
    updated = anchor[0] - 0.7 * (delta + 0.9 * moment)
    new_params = lax.all_gather(updated.astype(jnp.bfloat16), "group", axis=0, tiled=True)
    return (new_params, updated[None], moment[None])


def solution(mesh):
    in_specs = (
        P("group", "fsdp", None),
        P("group", "fsdp", None),
        P("group", "fsdp"),
        P("group", "fsdp", None),
        P("fsdp", "group", None),
        P("fsdp", "group", None),
    )
    out_specs = (P("fsdp", None), P("fsdp", "group", None), P("fsdp", "group", None))
    return jax.shard_map(local, mesh=mesh, in_specs=in_specs, out_specs=out_specs, check_vma=False)
```

profile of v0, /device:TPU:2, one launch (start us, length us, event | category | flops | bytes accessed | tf_op | source)
XLA Modules:
  0.0 399.6 jit_solution(1158466843580460970)
XLA Ops:
  7.2 0.0 all-gather.3.cloned.1.call-start
  7.9 1.8 bitcast_select_fusion
  9.7 0.0 all-gather.3.cloned.1.call-update
  9.7 4.0 copy.16
  13.7 13.5 %all-to-all-start = ((bf16[160,32,160]{0,2,1:T(8,128)(2,1)}), bf16[160,32,160]{0,2,1:T(8,128)(2,1)S(1)}, u32[]{:S(2)}, u32[]{:S(2)}) async-start(bf16[160,32,160]{0,2,1:T(8,128)(2,1)} %bitcast.49), calls=%async_computation | async-start | bytes 5242880 | tf_op jit(solution)/shard_map/all_to_all | solution.py:18
  27.1 0.0 all-reduce.3.cloned.1.call-start
  27.2 171.8 %psum.7 = f32[16]{0:T(128)S(1)} all-reduce(f32[16]{0:T(128)S(1)} %compare_select_fusion.1), channel_id=1, replica_groups=mesh['group'=16,'fsdp'=32] {'group','fsdp'}, use_global_device_ids=true, to_apply=%region_0.1 | all-reduce | flops 16 | bytes 128 | tf_op jit(solution)/shard_map/psum | solution.py:15
  199.0 0.6 fusion.7
  201.0 0.0 all-to-all-done
  201.0 3.0 copy.17
  204.0 0.0 copy-start.2
  204.0 5.5 %all_to_all.17 = bf16[5120,160]{0,1:T(8,128)(2,1)S(1)} reshape(bf16[32,160,160]{1,0,2:T(8,128)(2,1)} %copy.17) | data formatting | bytes 3276800 | tf_op jit(solution)/shard_map/all_to_all | solution.py:18
  209.5 0.0 copy-start
  209.5 0.0 copy-start.1
  209.6 0.0 all-gather.3.cloned.1.call-done
  209.6 0.0 copy-done.2
  209.6 7.4 %fusion.3 = f32[160,1024]{1,0:T(8,128)} fusion(bf16[5120,160]{0,1:T(8,128)(2,1)S(1)} %all_to_all.17, bf16[5120,1024]{1,0:T(8,128)(2,1)} %all-gather.3.cloned.1.call-done, bf16[1,160,1024]{2,1,0:T(8,128)(2,1)S(1)} %copy-done.2, f32[]{:T(128)} %get-tuple-element.13, f32[]{:T(128)S(6)} %div.10), kind=kOutput, calls=%fused_computation.4 | convolution fusion | flops 1678540800 | bytes 13107208 | tf_op jit(solution)/shard_map/dot_general | solution.py:19
  217.0 0.0 all-reduce.3.cloned.1.call-update
  217.0 1.3 dynamic-slice
  218.9 134.2 %all-reduce.3.cloned.1.call-done = f32[160,1024]{1,0:T(8,128)} async-done(((f32[160,1024]{1,0:T(8,128)}), f32[160,1024]{1,0:T(8,128)}) %all-reduce.3.cloned.1.call-update) | async-done | bytes 655376
  353.2 0.0 copy-done
  353.2 0.0 copy-done.1
  353.2 0.9 fusion.4
  354.1 36.5 %all-gather = bf16[16,10,1024]{2,1,0:T(8,128)(2,1)S(1)} all-gather(bf16[1,10,1024]{2,1,0:T(8,128)(2,1)S(1)} %get-tuple-element.16), channel_id=1, replica_groups=mesh['group'=16,'fsdp'=32] {'group'}, dimensions={0}, use_global_device_ids=true | all-gather | bytes 348160 | tf_op jit(solution)/shard_map/all_gather | solution.py:31
  390.6 0.8 reshape.20
  391.4 0.7 copy.19
  392.1 0.7 copy.20
  (2 shorter events, 0.0 us)
Async XLA Ops:
  7.2 202.4 %all-gather.3.cloned.1.call-start = ((), (), s32[]{:S(2)}) async-start(), calls=%async_computation.1 | async-start | bytes 10813440 | tf_op jit(solution)/shard_map/all_gather | solution.py:21
  13.7 187.3 %all-to-all-start = ((bf16[160,32,160]{0,2,1:T(8,128)(2,1)}), bf16[160,32,160]{0,2,1:T(8,128)(2,1)S(1)}, u32[]{:S(2)}, u32[]{:S(2)}) async-start(bf16[160,32,160]{0,2,1:T(8,128)(2,1)} %bitcast.49), calls=%async_computation | async-start | bytes 5242880 | tf_op jit(solution)/shard_map/all_to_all | solution.py:18
  27.1 326.0 %all-reduce.3.cloned.1.call-start = ((), (), s32[]{:S(2)}) async-start(), calls=%async_computation.2 | async-start | bytes 1310720
  204.0 5.6 %copy-start.2 = (bf16[1,160,1024]{2,1,0:T(8,128)(2,1)S(1)}, bf16[1,160,1024]{2,1,0:T(8,128)(2,1)}, u32[]{:S(2)}) copy-start(bf16[1,160,1024]{2,1,0:T(8,128)(2,1)} %param.9) | copy-start | bytes 983044
  209.5 143.6 %copy-start = (f32[1,10,1024]{2,0,1:T(1,128)S(1)}, f32[1,10,1024]{2,0,1:T(1,128)}, u32[]{:S(2)}) copy-start(f32[1,10,1024]{2,0,1:T(1,128)} %param.11) | copy-start | bytes 122884
  209.5 143.6 %copy-start.1 = (f32[1,10,1024]{2,0,1:T(1,128)S(1)}, f32[1,10,1024]{2,0,1:T(1,128)}, u32[]{:S(2)}) copy-start(f32[1,10,1024]{2,0,1:T(1,128)} %param.10) | copy-start | bytes 122884
Sparse Core Ops, SparseCore 0:
  11.7 144.2 all-gather.2
  217.1 135.9 all-reduce.2
where the time goes:
time: 400 us
  blocking collectives  208 us (52%)
  waiting for transfers between devices  134 us (34%)
  between operations  16.8 us (4%)
  local copies, waits for them, and re-layouts  16 us (4%)
  starting transfers between devices  13.5 us (3%)
  matrix products  7.41 us (2%)
    psum x1, blocking collectives, local(): counts_all = lax.psum(own_count, ('group', 'fsdp'))  172 us
    unnamed x3, waiting for transfers between devices  134 us
    all_gather x1, blocking collectives, local(): lax.all_gather(updated.astype(jnp.bfloat16), 'group', axis=0, tiled=True)  36.5 us
    all_to_all x1, starting transfers between devices, local(): lax.all_to_all(activations[0], 'fsdp', split_axis=1, concat_axis=0, tiled...  13.5 us
    all_to_all x2, local copies, waits for them, and re-layouts, local(): lax.all_to_all(activations[0], 'fsdp', split_axis=1, concat_axis=0, tiled...  8.55 us
  transfers between devices with their start and end apart: 3, of which 1 were waited for; matrix products, arithmetic and copies ran while one was open for 2% of the time, Pallas kernels for 0%

commit v1 on v0

v1 whole, which is shorter than its diff:
```python
import jax
import jax.numpy as jnp
from jax import lax
from jax.experimental import pallas as pl
from jax.experimental.pallas import tpu as pltpu
from jax.sharding import PartitionSpec as P

MESH = pl.DeviceIdType.MESH
BF, F32 = jnp.bfloat16, jnp.float32
SIZE = {"x": 4, "y": 8, "z": 8}
UNITS = ("xyz", "xzy", "yxz", "zxy", "zxy")
NU = len(UNITS)
TILE = (16, 128)
TOK, ROWS, COLS, LIN = 160, 160, 1024, 80
VMEM_LIMIT = 56_000_000


def coords():
    g, f = lax.axis_index("group"), lax.axis_index("fsdp")
    return {"x": (f // 2) % 4, "y": g // 2, "z": (f // 8) * 2 + g % 2, "c": f % 2}


def device(at):
    return (at["y"] * 2 + at["z"] % 2, (at["z"] // 2) * 8 + at["x"] * 2 + at["c"])


def peer(here, axis, step):
    n = SIZE[axis]
    return device({**here, axis: (here[axis] + step + n) % n})


def loop(n, body, start=0):
    def step(i, carry):
        body(i)
        return carry

    lax.fori_loop(start, n, step, 0)


def put(src, dst, ssem, rsem, to):
    return pltpu.make_async_remote_copy(
        src_ref=src, dst_ref=dst, send_sem=ssem, recv_sem=rsem, device_id=to, device_id_type=MESH
    )


class Ring:
    def __init__(self, here, sign, axis, part, far, near, fs, fr, ns, nr):
        self.here, self.sign, self.axis, self.part = here, sign, axis, part
        self.n, self.me = SIZE[axis], here[axis]
        self.far, self.near = far, near
        self.sems = (fs, fr, ns, nr)

    def _far(self, k):
        t = (self.me + self.sign * (self.n // 2 - k) + self.n) % self.n
        to = peer(self.here, self.axis, self.sign)
        return t, put(self.part.at[t], self.far.at[k], self.sems[0].at[k], self.sems[1].at[k], to)

    def _near(self, k):
        t = (self.me - self.sign * (self.n // 2 - 1 - k) + self.n) % self.n
        to = peer(self.here, self.axis, -self.sign)
        return t, put(self.part.at[t], self.near.at[k], self.sems[2].at[k], self.sems[3].at[k], to)

    def _add(self, t, got):
        def body(i):
            self.part[t, i] = (self.part[t, i].astype(F32) + got[i].astype(F32)).astype(BF)

        loop(self.part.shape[1], body)

    def send_far(self, k):
        t, copy = self._far(k)
        if k:
            self._far(k - 1)[1].wait_recv()
            self._add(t, self.far.at[k - 1])
        copy.start()

    def send_near(self, k):
        t, copy = self._near(k)
        if k:
            self._near(k - 1)[1].wait_recv()
            self._add(t, self.near.at[k - 1])
        copy.start()

    def finish(self):
        h = self.n // 2
        self._far(h - 1)[1].wait_recv()
        self._near(h - 2)[1].wait_recv()
        a, b = self.far.at[h - 1], self.near.at[h - 2]

        def body(i):
            total = self.part[self.me, i].astype(F32) + a[i].astype(F32) + b[i].astype(F32)
            self.part[self.me, i] = total.astype(BF)

        loop(self.part.shape[1], body)
        return self.part.at[self.me]

    def drain(self):
        for k in range(self.n // 2):
            self._far(k)[1].wait_send()
        for k in range(self.n // 2 - 1):
            self._near(k)[1].wait_send()


class Direct:
    def __init__(self, here, axis, part, slots, ss, rs):
        self.here, self.axis, self.part, self.slots = here, axis, part, slots
        self.n, self.me, self.ss, self.rs = SIZE[axis], here[axis], ss, rs

    def _copy(self, d):
        t = (self.me + d) % self.n
        to = peer(self.here, self.axis, d)
        return put(self.part.at[t], self.slots.at[d - 1], self.ss.at[d - 1], self.rs.at[d - 1], to)

    def start(self):
        loop(self.n, lambda d: self._copy(d).start(), 1)

    def arrive(self):
        loop(self.n, lambda d: self._copy(d).wait_recv(), 1)

    def total(self, i=None):
        at = (self.me,) if i is None else (self.me, i)
        acc = self.part[at].astype(F32)
        for d in range(self.n - 1):
            acc += self.slots[(d,) + at[1:]].astype(F32)
        return acc

    def drain(self):
        loop(self.n, lambda d: self._copy(d).wait_send(), 1)


def scratch():
    s = {}
    dma = pltpu.SemaphoreType.DMA
    s["a"], s["m"], s["lp"] = (pltpu.VMEM(v, BF) for v in ((TOK, 5120), (TOK, COLS), (ROWS, COLS)))
    s["anc"], s["mom"] = pltpu.VMEM((LIN, 128), F32), pltpu.VMEM((LIN, 128), F32)
    s["insem"] = dma((5,))
    s["at"] = pltpu.VMEM((2, 16, ROWS, TOK), BF)
    s["atp"] = pltpu.VMEM((16, ROWS, TOK), BF)
    s["mp"] = pltpu.VMEM((TOK, COLS), BF)
    s["exs"], s["exr"] = dma((3,)), dma((3,))
    s["cv"] = pltpu.VMEM((4, 8, 128), F32)
    s["cc"], s["cx"] = pltpu.VMEM((8, 128), F32), pltpu.VMEM((3, 8, 128), F32)
    s["cz"], s["cy"] = pltpu.VMEM((7, 8, 128), F32), pltpu.VMEM((7, 8, 128), F32)
    for k, n in (("cx", 3), ("cz", 7), ("cy", 7)):
        s[k + "s"], s[k + "r"] = dma((n,)), dma((n,))
    for u, order in enumerate(UNITS):
        n1, n2, n3 = (SIZE[k] for k in order)
        s[f"u{u}"] = pltpu.VMEM((n1, n2, n3) + TILE, BF)
        s[f"far{u}"] = pltpu.VMEM((n1 // 2, n2, n3) + TILE, BF)
        s[f"near{u}"] = pltpu.VMEM((n1 // 2 - 1, n2, n3) + TILE, BF)
        s[f"fs{u}"], s[f"fr{u}"] = dma((n1 // 2,)), dma((n1 // 2,))
        s[f"ns{u}"], s[f"nr{u}"] = dma((n1 // 2 - 1,)), dma((n1 // 2 - 1,))
        s[f"two{u}"] = pltpu.VMEM((n2 - 1, n3) + TILE, BF)
        s[f"ts{u}"], s[f"tr{u}"] = dma((n2 - 1,)), dma((n2 - 1,))
        s[f"v{u}"] = pltpu.VMEM((n3,) + TILE, BF)
        s[f"three{u}"] = pltpu.VMEM((n3 - 1,) + TILE, BF)
        s[f"hs{u}"], s[f"hr{u}"] = dma((n3 - 1,)), dma((n3 - 1,))
    s["base"] = pltpu.VMEM((16, LIN, 128), BF)
    s["basef"] = pltpu.VMEM((ROWS * 8, 128), F32)
    s["bs"], s["br"] = dma((15,)), dma((15,))
    s["ag"] = pltpu.VMEM((16, NU) + TILE, BF)
    s["as"], s["ar"] = dma((15,)), dma((15,))
    s["avg"] = pltpu.VMEM((ROWS * 8, 128), F32)
    return s


NAMES = tuple(scratch())


def kernel(live_ref, a_hbm, m_hbm, lp_hbm, anc_hbm, mom_hbm, np_ref, na_ref, nm_ref, *refs):
    s = dict(zip(NAMES, refs))
    anc_ref, mom_ref = s["anc"], s["mom"]
    here = coords()
    x, y, z, c = (here[k] for k in "xyzc")
    zl, g = z % 2, y * 2 + z % 2
    sign = 1 - 2 * c
    partner = device({**here, "c": 1 - c})

    def group_peer(j):
        other = (g + j) % 16
        return (other, lax.axis_index("fsdp"))

    bar = pltpu.get_barrier_semaphore()

    def greet(to):
        pl.semaphore_signal(bar, inc=1, device_id=to, device_id_type=MESH)

    greet(partner)
    loop(4, lambda d: greet(peer(here, "x", d)), 1)
    loop(8, lambda d: greet(peer(here, "z", d)), 1)
    loop(16, lambda j: greet(group_peer(j)), 1)

    wanted = ((a_hbm, s["a"]), (m_hbm, s["m"]), (lp_hbm, s["lp"]), (anc_hbm, anc_ref), (mom_hbm, mom_ref))
    loads = [pltpu.make_async_copy(src, dst, s["insem"].at[i]) for i, (src, dst) in enumerate(wanted)]
    for load in loads:
        load.start()

    live = live_ref[0, 0]
    s["cv"][0] = jnp.full((8, 128), live.astype(F32), F32)

    loads[1].wait()
    row = lax.broadcasted_iota(jnp.int32, (TOK, COLS), 0)
    s["m"][...] = jnp.where(row < live, s["m"][...].astype(F32), 0.0).astype(BF)
    loads[0].wait()

    def transpose(k):
        t = s["a"][:, pl.ds(pl.multiple_of(k * 640, 128), 640)].T
        for j in range(4):
            s["at"][j % 2, 2 * k + j // 2] = t[j * 160:(j + 1) * 160]

    loop(8, transpose)
    for load in loads[2:]:
        load.wait()
    s["base"][g] = (-0.33 * anc_ref[...] - 0.567 * mom_ref[...]).astype(BF)

    pl.semaphore_wait(bar, 1 + 3 + 7 + 15)

    ex = [put(s["cv"].at[0], s["cc"], s["exs"].at[2], s["exr"].at[2], partner),
          put(s["m"], s["mp"], s["exs"].at[1], s["exr"].at[1], partner),
          put(s["at"].at[1 - c], s["atp"], s["exs"].at[0], s["exr"].at[0], partner)]
    for copy in ex:
        copy.start()

    def base_copy(j):
        return put(s["base"].at[g], s["base"].at[g], s["bs"].at[j - 1], s["br"].at[j - 1], group_peer(j))

    def base_in(j):
        src = (g - j + 16) % 16
        return put(s["base"].at[src], s["base"].at[src], s["bs"].at[j - 1], s["br"].at[j - 1], group_peer(j))

    def count_copy(key, axis, d, k):
        return put(s["cv"].at[k], s[key].at[d - 1], s[key + "s"].at[d - 1], s[key + "r"].at[d - 1], peer(here, axis, d))

    ex[0].wait_recv()
    s["cv"][1] = s["cv"][0] + s["cc"][...]
    loop(4, lambda d: count_copy("cx", "x", d, 1).start(), 1)
    loop(16, lambda j: base_copy(j).start(), 1)

    rings, twos, threes = [], [], []
    for u, order in enumerate(UNITS):
        rings.append(Ring(here, sign, order[0], s[f"u{u}"], s[f"far{u}"], s[f"near{u}"],
                          s[f"fs{u}"], s[f"fr{u}"], s[f"ns{u}"], s[f"nr{u}"]))

    ex[1].wait_recv()
    ex[2].wait_recv()

    def block(dz, dx, own=None):
        bz, bx = (z // 2 + dz) % 4, (x + dx) % 4
        blk = bz * 4 + bx
        for h in range(2):
            cols = slice(h * 512, (h + 1) * 512)
            acc = jnp.dot(s["at"][c, blk], s["m"][:, cols], preferred_element_type=F32)
            acc += jnp.dot(s["atp"][blk], s["mp"][:, cols], preferred_element_type=F32)
            if own is not None:
                acc -= (2.0 * own) * s["lp"][:, cols].astype(F32)
            out = acc.astype(BF)
            for u, order in enumerate(UNITS):
                for q in range(2):
                    for t in range(4):
                        at = {"x": bx, "y": h * 4 + t, "z": bz * 2 + q}
                        s[f"u{u}"][at[order[0]], at[order[1]], at[order[2]]] = (
                            out[u * 32 + q * 16:u * 32 + q * 16 + 16, t * 128:(t + 1) * 128])

    loop(4, lambda i: block(2, i))
    for u in (3, 4):
        rings[u].send_far(0)

    loop(4, lambda d: count_copy("cx", "x", d, 1).wait_recv(), 1)
    s["cv"][2] = s["cv"][1] + s["cx"][0] + s["cx"][1] + s["cx"][2]
    loop(8, lambda d: count_copy("cz", "z", d, 2).start(), 1)

    loop(3, lambda i: block((i + 3) % 4, 2))
    for u in (0, 1):
        rings[u].send_far(0)
    loop(8, lambda i: block(jnp.maximum(3 - 2 * (i // 3), 0), jnp.maximum(3 - 2 * (i % 3), 0)))
    for u in (0, 1):
        rings[u].send_near(0)

    loop(8, lambda d: count_copy("cz", "z", d, 2).wait_recv(), 1)
    cz = s["cz"]
    count = s["cv"][2] + cz[1] + cz[3] + cz[5]
    s["cv"][3] = count + cz[0] + cz[2] + cz[4] + cz[6]
    loop(8, lambda d: count_copy("cy", "y", d, 3).start(), 1)
    block(0, 0, count[0:1, 0:1])
    rings[2].send_far(0)
    for u in (2, 3, 4):
        rings[u].send_near(0)

    def second(u):
        part = rings[u].finish()
        d = Direct(here, UNITS[u][1], part, s[f"two{u}"], s[f"ts{u}"], s[f"tr{u}"])
        d.start()
        twos.append(d)
        return d

    def third(u, d):
        d.arrive()

        def body(i):
            s[f"v{u}"][i] = d.total(i).astype(BF)

        loop(SIZE[UNITS[u][2]], body)
        e = Direct(here, UNITS[u][2], s[f"v{u}"], s[f"three{u}"], s[f"hs{u}"], s[f"hr{u}"])
        e.start()
        threes.append(e)
        return e

    rings[2].send_far(1)
    for u in (3, 4):
        rings[u].send_far(1)
    rings[2].send_near(1)
    for u in (3, 4):
        rings[u].send_near(1)
    rings[2].send_far(2)
    rings[2].send_near(2)
    for u in (0, 1):
        rings[u].send_far(1)
    rings[2].send_far(3)
    for u in (3, 4):
        rings[u].send_far(2)
        rings[u].send_near(2)
    d2 = second(2)
    loop(8, lambda d: count_copy("cy", "y", d, 3).wait_recv(), 1)
    total = s["cv"][3]
    for k in range(7):
        total += s["cy"][k]
    loop(16, lambda j: base_in(j).wait_recv(), 1)

    def widen(j):
        s["basef"][pl.ds(pl.multiple_of(j * LIN, 8), LIN), :] = s["base"][j].astype(F32)

    loop(16, widen)
    scale = (-0.5 / total)[0:1, 0:1]

    for u in (3, 4):
        rings[u].send_far(3)
    d0, d1 = second(0), second(1)
    e2 = third(2, d2)
    d3, d4 = second(3), second(4)
    e0, e1 = third(0, d0), third(1, d1)
    e3, e4 = third(3, d3), third(4, d4)

    for u, e in ((2, e2), (0, e0), (1, e1), (3, e3), (4, e4)):
        e.arrive()
        s["ag"][g, u] = (scale * e.total()).astype(BF)

    def ag_copy(j):
        return put(s["ag"].at[g], s["ag"].at[g], s["as"].at[j - 1], s["ar"].at[j - 1], group_peer(j))

    def ag_in(j):
        src = (g - j + 16) % 16
        return put(s["ag"].at[src], s["ag"].at[src], s["as"].at[j - 1], s["ar"].at[j - 1], group_peer(j))

    loop(16, lambda j: ag_copy(j).start(), 1)

    for r in rings:
        r.drain()
    for d in twos + threes:
        d.drain()
    for copy in ex:
        copy.wait_send()
    for key, axis, k, n in (("cx", "x", 1, 4), ("cz", "z", 2, 8), ("cy", "y", 3, 8)):
        loop(n, lambda d, key=key, axis=axis, k=k: count_copy(key, axis, d, k).wait_send(), 1)
    loop(16, lambda j: base_copy(j).wait_send(), 1)

    loop(16, lambda j: ag_in(j).wait_recv(), 1)
    for yy in range(8):
        for q in range(2):
            for u in range(NU):
                r0 = u * 32 + q * 16
                avg = s["ag"][yy * 2 + q, u].astype(F32)
                s["avg"][pl.ds(r0 * 8 + yy, 16, stride=8), :] = avg
                base = s["basef"][pl.ds(r0 * 8 + yy, 16, stride=8), :]
                np_ref[r0:r0 + 16, yy * 128:(yy + 1) * 128] = (base + 1.33 * avg).astype(BF)
    own = s["avg"][pl.ds(pl.multiple_of(g * LIN, 8), LIN), :]
    anc = anc_ref[...]
    delta = anc - own
    moment = 0.9 * mom_ref[...] + delta
    nm_ref[...] = moment
    na_ref[...] = anc - 0.7 * (delta + 0.9 * moment)
    loop(16, lambda j: ag_copy(j).wait_send(), 1)


def local(activations, cotangent, live, local_params, anchor, momentum):
    vmem = pl.BlockSpec(memory_space=pltpu.VMEM)
    hbm = pl.BlockSpec(memory_space=pltpu.HBM)
    new_params, new_anchor, new_momentum = pl.pallas_call(
        kernel,
        name="outer_step",
        out_shape=(
            jax.ShapeDtypeStruct((ROWS, COLS), BF),
            jax.ShapeDtypeStruct((LIN, 128), F32),
            jax.ShapeDtypeStruct((LIN, 128), F32),
        ),
        in_specs=[pl.BlockSpec(memory_space=pltpu.SMEM), hbm, hbm, hbm, hbm, hbm],
        out_specs=(vmem, vmem, vmem),
        scratch_shapes=list(scratch().values()),
        compiler_params=pltpu.CompilerParams(
            collective_id=0, has_side_effects=True, vmem_limit_bytes=VMEM_LIMIT
        ),
    )(live, activations[0], cotangent[0], local_params[0], anchor.reshape(LIN, 128), momentum.reshape(LIN, 128))
    return new_params, new_anchor.reshape(1, 10, COLS), new_momentum.reshape(1, 10, COLS)


def solution(mesh):
    in_specs = (
        P("group", "fsdp", None),
        P("group", "fsdp", None),
        P("group", "fsdp"),
        P("group", "fsdp", None),
        P("fsdp", "group", None),
        P("fsdp", "group", None),
    )
    out_specs = (P("fsdp", None), P("fsdp", "group", None), P("fsdp", "group", None))
    return jax.shard_map(local, mesh=mesh, in_specs=in_specs, out_specs=out_specs, check_vma=False)
```

time: 400 us -> 82.5 us (0.21)
  the two profiles are of different devices: /device:TPU:2 before, /device:TPU:64 now
where the time goes in v1:
time: 82.5 us; the launch traced here: 82.2 us
  Pallas kernels  77.4 us (94%)
  local copies, waits for them, and re-layouts  3.51 us (4%)
  between operations  1.3 us (2%)
    pallas_call x1, Pallas kernels, local(): pl.pallas_call(kernel, name='outer_step', out_shape=(jax.ShapeDtypeStruct...  77.4 us
    unnamed x7, local copies, waits for them, and re-layouts  3.51 us

profile of v1, /device:TPU:64, one launch (start us, length us, event | category | flops | bytes accessed | tf_op | source)
XLA Modules:
  0.0 82.2 jit_solution(4129935603884919117)
XLA Ops:
  1.3 0.0 copy-start
  1.3 0.8 copy-done
  2.1 0.0 copy-start.1
  2.1 0.8 copy-done.1
  2.8 77.4 %outer_step.1 = (bf16[160,1024]{1,0:T(8,128)(2,1)S(1)}, f32[80,128]{1,0:T(8,128)S(1)}, f32[80,128]{1,0:T(8,128)S(1)}) custom-call(s32[1,1]{1,0:T(1,128)S(6)} %copy.16.live_ref, bf16[160,5120]{1,0:T(8,128)(2,1)} %bitcast.11, bf16[160,1024]{1,0:T(8,128)(2,1)} %bitcast.12, bf16[160,1024]{1,0:T(8,128)(2,1)} %bitcast.13, f32[80,128]{1,0:T(8,128)S(1)} %bitcast.9, ...), custom_call_target="tpu_custom_call" | custom-call | tf_op jit(solution)/shard_map/outer_step/pallas_call | solution.py:386
  80.3 0.7 copy.17
  81.0 0.6 copy.18
  81.6 0.6 copy.19
Async XLA Ops:
  1.3 0.8 copy-start
  2.1 0.8 copy-start.1

commit v2 on v1

v2 whole, which is shorter than its diff:
```python
import jax
import jax.numpy as jnp
from jax import lax
from jax.experimental import pallas as pl
from jax.experimental.pallas import tpu as pltpu
from jax.sharding import PartitionSpec as P

MESH = pl.DeviceIdType.MESH
BF, F32 = jnp.bfloat16, jnp.float32
SIZE = {"x": 4, "y": 8, "z": 8, "p": 8, "q": 8}
UNITS = ("xqp", "xpq", "yxz", "zxy", "pxq")
HALVES = 1
WAVES = ((0, 1, 2, 3, 4),)
PLAN = ("m0", "f00", "f10", "x", "m1", "n00", "n10", "m2", "m3", "f30", "n30", "t", "o", "f20", "n20", "f40", "n40",
        "q0", "f31", "n31", "f21", "n21", "f41", "n41", "f01", "q1", "f32", "n32", "f22", "n22", "f42", "n42",
        "f11", "s0", "q2", "c", "f33", "f23", "f43", "q3", "s1", "s2", "s3", "s4", "b",
        "h0", "h1", "h2", "h3", "h4", "w0", "d", "e0")
NU = len(UNITS)
TILE = (16, 128)
TOK, ROWS, COLS, LIN = 160, 160, 1024, 80
VMEM_LIMIT = 56_000_000


def coords():
    g, f = lax.axis_index("group"), lax.axis_index("fsdp")
    return with_pq({"x": (f // 2) % 4, "y": g // 2, "z": (f // 8) * 2 + g % 2, "c": f % 2})


def with_pq(at):
    c, y, z = at["c"], at["y"], at["z"]
    return {**at, "p": z + c * (y - z), "q": y + c * (z - y)}


def device(at):
    return (at["y"] * 2 + at["z"] % 2, (at["z"] // 2) * 8 + at["x"] * 2 + at["c"])


def peer(here, axis, step):
    n, c = SIZE[axis], here["c"]
    if axis in "pq":
        dy = step * (c if axis == "p" else 1 - c)
        return device({**here, "y": (here["y"] + dy + 8) % 8, "z": (here["z"] + step - dy + 8) % 8})
    return device({**here, axis: (here[axis] + step + n) % n})


def loop(n, body, start=0):
    def step(i, carry):
        body(i)
        return carry

    lax.fori_loop(start, n, step, 0)


def put(src, dst, ssem, rsem, to):
    return pltpu.make_async_remote_copy(
        src_ref=src, dst_ref=dst, send_sem=ssem, recv_sem=rsem, device_id=to, device_id_type=MESH
    )


class Ring:
    def __init__(self, here, sign, axis, part, far, near, fs, fr, ns, nr):
        self.here, self.sign, self.axis, self.part = here, sign, axis, part
        self.n, self.me = SIZE[axis], here[axis]
        self.far, self.near = far, near
        self.sems = (fs, fr, ns, nr)
        self.width = part.shape[1] // HALVES

    def _cut(self, h):
        return slice(h * self.width, (h + 1) * self.width)

    def _far(self, k, h):
        t = (self.me + self.sign * (self.n // 2 - k) + self.n) % self.n
        to = peer(self.here, self.axis, self.sign)
        src, dst = self.part.at[t, self._cut(h)], self.far.at[k, self._cut(h)]
        return t, put(src, dst, self.sems[0].at[k, h], self.sems[1].at[k, h], to)

    def _near(self, k, h):
        t = (self.me - self.sign * (self.n // 2 - 1 - k) + self.n) % self.n
        to = peer(self.here, self.axis, -self.sign)
        src, dst = self.part.at[t, self._cut(h)], self.near.at[k, self._cut(h)]
        return t, put(src, dst, self.sems[2].at[k, h], self.sems[3].at[k, h], to)

    def _add(self, t, got, h):
        cut = self._cut(h)
        self.part[t, cut] = self.part[t, cut] + got[cut]

    def send_far(self, k, h):
        t, copy = self._far(k, h)
        if k:
            self._far(k - 1, h)[1].wait_recv()
            self._add(t, self.far.at[k - 1], h)
        copy.start()

    def send_near(self, k, h):
        t, copy = self._near(k, h)
        if k:
            self._near(k - 1, h)[1].wait_recv()
            self._add(t, self.near.at[k - 1], h)
        copy.start()

    def finish(self):
        n = self.n // 2
        a, b = self.far.at[n - 1], self.near.at[n - 2]

        def body(i):
            total = self.part[self.me, i].astype(F32) + a[i].astype(F32) + b[i].astype(F32)
            self.part[self.me, i] = total.astype(BF)

        for h in range(HALVES):
            self._near(n - 2, h)[1].wait_recv()
            self._far(n - 1, h)[1].wait_recv()
            loop((h + 1) * self.width, body, h * self.width)
        return self.part.at[self.me]

    def drain(self):
        for h in range(HALVES):
            for k in range(self.n // 2):
                self._far(k, h)[1].wait_send()
            for k in range(self.n // 2 - 1):
                self._near(k, h)[1].wait_send()


class Direct:
    def __init__(self, here, axis, part, slots, ss, rs):
        self.here, self.axis, self.part, self.slots = here, axis, part, slots
        self.n, self.me, self.ss, self.rs = SIZE[axis], here[axis], ss, rs

    def _copy(self, d):
        t = (self.me + d) % self.n
        to = peer(self.here, self.axis, d)
        return put(self.part.at[t], self.slots.at[d - 1], self.ss.at[d - 1], self.rs.at[d - 1], to)

    def start(self):
        loop(self.n, lambda d: self._copy(d).start(), 1)

    def arrive(self):
        loop(self.n, lambda d: self._copy(d).wait_recv(), 1)

    def total(self, i=None):
        at = (self.me,) if i is None else (self.me, i)
        acc = self.part[at].astype(F32)
        for d in range(self.n - 1):
            acc += self.slots[(d,) + at[1:]].astype(F32)
        return acc

    def drain(self):
        loop(self.n, lambda d: self._copy(d).wait_send(), 1)


def scratch():
    s = {}
    dma = pltpu.SemaphoreType.DMA
    s["a"], s["m"], s["lp"] = (pltpu.VMEM(v, BF) for v in ((TOK, 5120), (TOK, COLS), (ROWS, COLS)))
    s["anc"], s["mom"] = pltpu.VMEM((LIN, 128), F32), pltpu.VMEM((LIN, 128), F32)
    s["insem"] = dma((6,))
    s["at"] = pltpu.VMEM((2, 4, 4 * ROWS, TOK), BF)
    s["atp"] = pltpu.VMEM((4, 4 * ROWS, TOK), BF)
    s["live"] = pltpu.VMEM((1, 1), jnp.int32)
    s["mp"] = pltpu.VMEM((TOK, COLS), BF)
    s["exs"], s["exr"] = dma((6,)), dma((6,))
    s["cv"] = pltpu.VMEM((4, 8, 128), F32)
    s["cc"], s["cx"] = pltpu.VMEM((8, 128), F32), pltpu.VMEM((3, 8, 128), F32)
    s["cz"], s["cy"] = pltpu.VMEM((7, 8, 128), F32), pltpu.VMEM((7, 8, 128), F32)
    for k, n in (("cx", 3), ("cz", 7), ("cy", 7)):
        s[k + "s"], s[k + "r"] = dma((n,)), dma((n,))
    for u, order in enumerate(UNITS):
        n1, n2, n3 = (SIZE[k] for k in order)
        s[f"u{u}"] = pltpu.VMEM((n1, n2, n3) + TILE, BF)
        s[f"far{u}"] = pltpu.VMEM((n1 // 2, n2, n3) + TILE, BF)
        s[f"near{u}"] = pltpu.VMEM((n1 // 2 - 1, n2, n3) + TILE, BF)
        s[f"fs{u}"], s[f"fr{u}"] = dma((n1 // 2, HALVES)), dma((n1 // 2, HALVES))
        s[f"ns{u}"], s[f"nr{u}"] = dma((n1 // 2 - 1, HALVES)), dma((n1 // 2 - 1, HALVES))
        s[f"two{u}"] = pltpu.VMEM((n2 - 1, n3) + TILE, BF)
        s[f"ts{u}"], s[f"tr{u}"] = dma((n2 - 1,)), dma((n2 - 1,))
        s[f"v{u}"] = pltpu.VMEM((n3,) + TILE, BF)
        s[f"three{u}"] = pltpu.VMEM((n3 - 1,) + TILE, BF)
        s[f"hs{u}"], s[f"hr{u}"] = dma((n3 - 1,)), dma((n3 - 1,))
    s["base"] = pltpu.VMEM((16, LIN, 128), BF)
    s["basef"] = pltpu.VMEM((ROWS * 8, 128), F32)
    s["bs"], s["br"] = dma((8,)), dma((8,))
    for w, units in enumerate(WAVES):
        s[f"ag{w}"] = pltpu.VMEM((16, len(units)) + TILE, BF)
        s[f"as{w}"], s[f"ar{w}"] = dma((15,)), dma((15,))
    s["avg"] = pltpu.VMEM((ROWS * 8, 128), F32)
    return s


NAMES = tuple(scratch())


def kernel(live_hbm, a_hbm, m_hbm, lp_hbm, anc_hbm, mom_hbm, np_ref, na_ref, nm_ref, *refs):
    s = dict(zip(NAMES, refs))
    anc_ref, mom_ref = s["anc"], s["mom"]
    here = coords()
    x, y, z, c = (here[k] for k in "xyzc")
    zl, g = z % 2, y * 2 + z % 2
    sign = 1 - 2 * c
    partner = device({**here, "c": 1 - c})

    def group_peer(j):
        other = (g + j) % 16
        return (other, lax.axis_index("fsdp"))

    bar = pltpu.get_barrier_semaphore()

    def greet(to):
        pl.semaphore_signal(bar, inc=1, device_id=to, device_id_type=MESH)

    greet(partner)
    loop(4, lambda d: greet(peer(here, "x", d)), 1)
    loop(8, lambda d: greet(peer(here, "z", d)), 1)
    loop(16, lambda j: greet(group_peer(j)), 1)

    wanted = ((live_hbm, s["live"]), (m_hbm, s["m"]), (a_hbm, s["a"]),
              (lp_hbm, s["lp"]), (anc_hbm, anc_ref), (mom_hbm, mom_ref))
    loads = [pltpu.make_async_copy(src, dst, s["insem"].at[i]) for i, (src, dst) in enumerate(wanted)]
    for load in loads:
        load.start()

    loads[0].wait()
    live = s["live"][...]
    s["cv"][0] = jnp.broadcast_to(live.astype(F32), (8, 128))
    loads[1].wait()
    row = lax.broadcasted_iota(jnp.int32, (TOK, COLS), 0)
    s["m"][...] = jnp.where(row < live, s["m"][...].astype(F32), 0.0).astype(BF)
    loads[2].wait()

    def transpose(k):
        t = s["a"][:, pl.ds(pl.multiple_of(k * 640, 128), 640)].T
        for j in range(4):
            at = pl.multiple_of((k % 2) * 320 + (j // 2) * 160, 16)
            s["at"][j % 2, k // 2, pl.ds(at, 160)] = t[j * 160:(j + 1) * 160]

    loop(8, transpose)
    for load in loads[3:]:
        load.wait()
    s["base"][g] = (-0.33 * anc_ref[...] - 0.567 * mom_ref[...]).astype(BF)

    pl.semaphore_wait(bar, 1 + 3 + 7 + 15)

    def rows_of(bx):
        return pl.ds(pl.multiple_of(bx * ROWS, 16), ROWS)

    def ex_copy(i, bx):
        rows = rows_of(bx)
        return put(s["at"].at[1 - c, :, rows], s["atp"].at[:, rows], s["exs"].at[2 + i], s["exr"].at[2 + i], partner)

    ex = [put(s["cv"].at[0], s["cc"], s["exs"].at[0], s["exr"].at[0], partner),
          put(s["m"], s["mp"], s["exs"].at[1], s["exr"].at[1], partner)]
    ex += [ex_copy(i, (x + dx + 4) % 4) for i, dx in enumerate((2, sign, -sign, 0))]
    for copy in ex[:4]:
        copy.start()

    zpartner = device({**here, "z": z + 1 - 2 * zl})
    base_z = put(s["base"].at[g], s["base"].at[g], s["bs"].at[7], s["br"].at[7], zpartner)

    def base_ring(k, way):
        pair = s["base"].at[pl.ds(2 * ((y - way * sign * k + 8) % 8), 2)]
        i = k if way > 0 else 4 + k
        return put(pair, pair, s["bs"].at[i], s["br"].at[i], peer(here, "y", way * sign))

    def base_step(k):
        if k == 0:
            base_z.wait_recv()
        else:
            base_ring(k - 1, 1).wait_recv()
            base_ring(k - 1, -1).wait_recv()
        base_ring(k, 1).start()
        if k < 3:
            base_ring(k, -1).start()

    def count_copy(key, axis, d, k):
        return put(s["cv"].at[k], s[key].at[d - 1], s[key + "s"].at[d - 1], s[key + "r"].at[d - 1], peer(here, axis, d))

    ex[0].wait_recv()
    s["cv"][1] = s["cv"][0] + s["cc"][...]
    loop(4, lambda d: count_copy("cx", "x", d, 1).start(), 1)
    base_z.start()

    rings = []
    for u, order in enumerate(UNITS):
        rings.append(Ring(here, sign, order[0], s[f"u{u}"], s[f"far{u}"], s[f"near{u}"],
                          s[f"fs{u}"], s[f"fr{u}"], s[f"ns{u}"], s[f"nr{u}"]))


    def store(out, bz, bx, r0, t0, width):
        for u, order in enumerate(UNITS):
            for q in range(2):
                for t in range(width):
                    at = with_pq({"x": bx, "y": t0 + t, "z": bz * 2 + q, "c": c})
                    r = r0 + u * 32 + q * 16
                    s[f"u{u}"][at[order[0]], at[order[1]], at[order[2]]] = out[r:r + 16, t * 128:(t + 1) * 128]

    def multiply(i):
        bx = (x + (2, -sign, sign, 0)[i] + 4) % 4
        rows = rows_of(bx)
        if i == 0:
            ex[1].wait_recv()
        ex_copy(i, bx).wait_recv()
        if i < 2:
            ex[4 + i].start()
        mine = s["at"][c, :, rows, :].reshape(4 * ROWS, TOK)
        theirs = s["atp"][:, rows, :].reshape(4 * ROWS, TOK)
        for h in range(4):
            cols = slice(h * 256, (h + 1) * 256)
            acc = jnp.dot(mine, s["m"][:, cols], preferred_element_type=F32)
            acc += jnp.dot(theirs, s["mp"][:, cols], preferred_element_type=F32)
            out = acc.astype(BF)
            for bz in range(4):
                store(out, bz, bx, bz * ROWS, h * 2, 2)

    def multiply_own(weight):
        rows = rows_of(x)
        for h in range(4):
            cols = slice(h * 256, (h + 1) * 256)
            acc = jnp.dot(s["at"][c, z // 2, rows], s["m"][:, cols], preferred_element_type=F32)
            acc += jnp.dot(s["atp"][z // 2, rows], s["mp"][:, cols], preferred_element_type=F32)
            acc -= weight * s["lp"][:, cols].astype(F32)
            store(acc.astype(BF), z // 2, x, 0, h * 2, 2)

    def far(u, k, h=None):
        for i in range(HALVES) if h is None else (h,):
            rings[u].send_far(k, i)

    def near(u, k, h=None):
        for i in range(HALVES) if h is None else (h,):
            rings[u].send_near(k, i)

    def second(u):
        part = rings[u].finish()
        d = Direct(here, UNITS[u][1], part, s[f"two{u}"], s[f"ts{u}"], s[f"tr{u}"])
        d.start()
        twos[u] = d

    def third(u):
        d = twos[u]
        d.arrive()

        def body(i):
            s[f"v{u}"][i] = d.total(i).astype(BF)

        loop(SIZE[UNITS[u][2]], body)
        e = Direct(here, UNITS[u][2], s[f"v{u}"], s[f"three{u}"], s[f"hs{u}"], s[f"hr{u}"])
        e.start()
        threes[u] = e

    def wave_send(w, total):
        for i, u in enumerate(WAVES[w]):
            threes[u].arrive()
            s[f"ag{w}"][g, i] = (total * threes[u].total()).astype(BF)
        for j in (8, 7, 9, 6, 10, 5, 11, 4, 12, 3, 13, 2, 14, 1, 15):
            ag_copy(w, j).start()

    def ag_copy(w, j):
        mine = s[f"ag{w}"].at[g]
        return put(mine, mine, s[f"as{w}"].at[j - 1], s[f"ar{w}"].at[j - 1], group_peer(j))

    def ag_in(w, j):
        theirs = s[f"ag{w}"].at[(g - j + 16) % 16]
        return put(theirs, theirs, s[f"as{w}"].at[j - 1], s[f"ar{w}"].at[j - 1], group_peer(j))

    def wave_end(w):
        loop(16, lambda j: ag_in(w, j).wait_recv(), 1)
        for i, u in enumerate(WAVES[w]):
            for yy in range(8):
                for q in range(2):
                    r0 = u * 32 + q * 16
                    avg = s[f"ag{w}"][yy * 2 + q, i].astype(F32)
                    s["avg"][pl.ds(r0 * 8 + yy, 16, stride=8), :] = avg
                    base = s["basef"][pl.ds(r0 * 8 + yy, 16, stride=8), :]
                    np_ref[r0:r0 + 16, yy * 128:(yy + 1) * 128] = (base + 1.33 * avg).astype(BF)

    twos, threes, known = {}, {}, {}

    def counts_x():
        loop(4, lambda d: count_copy("cx", "x", d, 1).wait_recv(), 1)
        s["cv"][2] = s["cv"][1] + s["cx"][0] + s["cx"][1] + s["cx"][2]
        loop(8, lambda d: count_copy("cz", "z", d, 2).start(), 1)

    def counts():
        loop(8, lambda d: count_copy("cz", "z", d, 2).wait_recv(), 1)
        cz = s["cz"]
        known["count"] = s["cv"][2] + cz[1] + cz[3] + cz[5]
        s["cv"][3] = known["count"] + cz[0] + cz[2] + cz[4] + cz[6]
        loop(8, lambda d: count_copy("cy", "y", d, 3).start(), 1)

    def total_count():
        loop(8, lambda d: count_copy("cy", "y", d, 3).wait_recv(), 1)
        total = s["cv"][3]
        for k in range(7):
            total += s["cy"][k]
        known["scale"] = (-0.5 / total)[0:1, 0:1]

    def base_rows():
        base_ring(3, 1).wait_recv()

        def widen(j):
            s["basef"][pl.ds(pl.multiple_of(j * LIN, 8), LIN), :] = s["base"][j].astype(F32)

        loop(16, widen)

    def drain():
        for r in rings:
            r.drain()
        for d in [*twos.values(), *threes.values()]:
            d.drain()
        for copy in ex:
            copy.wait_send()
        for key, axis, k, n in (("cx", "x", 1, 4), ("cz", "z", 2, 8), ("cy", "y", 3, 8)):
            loop(n, lambda d, key=key, axis=axis, k=k: count_copy(key, axis, d, k).wait_send(), 1)
        base_z.wait_send()
        for k in range(4):
            base_ring(k, 1).wait_send()
        for k in range(3):
            base_ring(k, -1).wait_send()

    steps = {
        "m": multiply, "q": base_step,
        "x": counts_x, "t": counts, "c": total_count, "b": base_rows, "d": drain,
        "o": lambda: multiply_own(2.0 * known["count"][0:1, 0:1]),
        "f": far, "n": near, "s": second, "h": third,
        "w": lambda w: wave_send(w, known["scale"]), "e": wave_end,
    }
    for step in PLAN:
        steps[step[0]](*(int(v) for v in step[1:]))

    own = s["avg"][pl.ds(pl.multiple_of(g * LIN, 8), LIN), :]
    anc = anc_ref[...]
    delta = anc - own
    moment = 0.9 * mom_ref[...] + delta
    nm_ref[...] = moment
    na_ref[...] = anc - 0.7 * (delta + 0.9 * moment)
    for w in range(len(WAVES)):
        loop(16, lambda j, w=w: ag_copy(w, j).wait_send(), 1)


def local(activations, cotangent, live, local_params, anchor, momentum):
    vmem = pl.BlockSpec(memory_space=pltpu.VMEM)
    hbm = pl.BlockSpec(memory_space=pltpu.HBM)
    new_params, new_anchor, new_momentum = pl.pallas_call(
        kernel,
        name="outer_step",
        out_shape=(
            jax.ShapeDtypeStruct((ROWS, COLS), BF),
            jax.ShapeDtypeStruct((LIN, 128), F32),
            jax.ShapeDtypeStruct((LIN, 128), F32),
        ),
        in_specs=[hbm] * 6,
        out_specs=(vmem, vmem, vmem),
        scratch_shapes=list(scratch().values()),
        compiler_params=pltpu.CompilerParams(
            collective_id=0, has_side_effects=True, vmem_limit_bytes=VMEM_LIMIT
        ),
    )(live, activations[0], cotangent[0], local_params[0], anchor.reshape(LIN, 128), momentum.reshape(LIN, 128))
    return new_params, new_anchor.reshape(1, 10, COLS), new_momentum.reshape(1, 10, COLS)


def solution(mesh):
    in_specs = (
        P("group", "fsdp", None),
        P("group", "fsdp", None),
        P("group", "fsdp"),
        P("group", "fsdp", None),
        P("fsdp", "group", None),
        P("fsdp", "group", None),
    )
    out_specs = (P("fsdp", None), P("fsdp", "group", None), P("fsdp", "group", None))
    return jax.shard_map(local, mesh=mesh, in_specs=in_specs, out_specs=out_specs, check_vma=False)
```

time: 82.5 us -> 73.1 us (0.89)
  the two profiles are of different devices: /device:TPU:64 before, /device:TPU:8 now
where the time goes in v2:
time: 73.1 us; the launch traced here: 72.8 us
  Pallas kernels  68 us (93%)
  local copies, waits for them, and re-layouts  3.51 us (5%)
  between operations  1.3 us (2%)
    pallas_call x1, Pallas kernels, local(): pl.pallas_call(kernel, name='outer_step', out_shape=(jax.ShapeDtypeStruct...  68 us
    unnamed x7, local copies, waits for them, and re-layouts  3.51 us

profile of v2, /device:TPU:8, one launch (start us, length us, event | category | flops | bytes accessed | tf_op | source)
XLA Modules:
  0.0 72.8 jit_solution(17634245330171549980)
XLA Ops:
  1.3 0.0 copy-start
  1.3 0.8 %copy-done = f32[1,10,1024]{2,0,1:T(1,128)S(1)} copy-done((f32[1,10,1024]{2,0,1:T(1,128)S(1)}, f32[1,10,1024]{2,0,1:T(1,128)}, u32[]{:S(2)}) %copy-start) | copy-done | bytes 40984
  2.1 0.0 copy-start.1
  2.1 0.8 %copy-done.1 = f32[1,10,1024]{2,0,1:T(1,128)S(1)} copy-done((f32[1,10,1024]{2,0,1:T(1,128)S(1)}, f32[1,10,1024]{2,0,1:T(1,128)}, u32[]{:S(2)}) %copy-start.1) | copy-done | bytes 40984
  2.8 68.0 %outer_step.1 = (bf16[160,1024]{1,0:T(8,128)(2,1)S(1)}, f32[80,128]{1,0:T(8,128)S(1)}, f32[80,128]{1,0:T(8,128)S(1)}) custom-call(s32[1,1]{1,0:T(1,128)S(6)} %copy.16.live_hbm, bf16[160,5120]{1,0:T(8,128)(2,1)} %bitcast.11, bf16[160,1024]{1,0:T(8,128)(2,1)} %bitcast.12, bf16[160,1024]{1,0:T(8,128)(2,1)} %bitcast.13, f32[80,128]{1,0:T(8,128)S(1)} %bitcast.9, ...), custom_call_target="tpu_custom_call" | custom-call | tf_op jit(solution)/shard_map/outer_step/pallas_call | solution.py:440
  70.8 0.7 copy.17
  71.5 0.6 copy.18
  72.2 0.6 copy.19
Async XLA Ops:
  1.3 0.8 %copy-start = (f32[1,10,1024]{2,0,1:T(1,128)S(1)}, f32[1,10,1024]{2,0,1:T(1,128)}, u32[]{:S(2)}) copy-start(f32[1,10,1024]{2,0,1:T(1,128)} %param.10) | copy-start | bytes 122884
  2.1 0.8 %copy-start.1 = (f32[1,10,1024]{2,0,1:T(1,128)S(1)}, f32[1,10,1024]{2,0,1:T(1,128)}, u32[]{:S(2)}) copy-start(f32[1,10,1024]{2,0,1:T(1,128)} %param.11) | copy-start | bytes 122884

commit v3 on v2

--- a/solution.py
+++ b/solution.py
@@ -8,15 +8,21 @@
 MESH = pl.DeviceIdType.MESH
 BF, F32 = jnp.bfloat16, jnp.float32
 SIZE = {"x": 4, "y": 8, "z": 8, "p": 8, "q": 8}
-UNITS = ("xqp", "xpq", "yxz", "zxy", "pxq")
+PARTS = (("xqp", (0,)), ("xpq", (1,)), ("pxq", (2,)), ("qxp", (3,)), ("pxq", (4,)))
+LAST = (("p", (0, 3)), ("q", (1, 2, 4)))
+UNITS = tuple(u for _, parts in LAST for p in parts for u in PARTS[p][1])
+NU = len(UNITS)
 HALVES = 1
-WAVES = ((0, 1, 2, 3, 4),)
-PLAN = ("m0", "f00", "f10", "x", "m1", "n00", "n10", "m2", "m3", "f30", "n30", "t", "o", "f20", "n20", "f40", "n40",
-        "q0", "f31", "n31", "f21", "n21", "f41", "n41", "f01", "q1", "f32", "n32", "f22", "n22", "f42", "n42",
-        "f11", "s0", "q2", "c", "f33", "f23", "f43", "q3", "s1", "s2", "s3", "s4", "b",
-        "h0", "h1", "h2", "h3", "h4", "w0", "d", "e0")
-NU = len(UNITS)
-TILE = (16, 128)
+PLAN = ("m0", "f00", "f10", "x", "m1", "n00", "n10", "m2", "m3", "t", "o",
+        "f30", "n30", "f20", "n20", "f40", "n40", "q0", "f31", "n31", "f21", "n21", "f41", "n41", "f01", "q1",
+        "f32", "n32", "f22", "n22", "f42", "n42", "f11", "s0", "q2", "f33", "f23", "f43", "q3",
+        "s1", "s2", "s3", "s4", "c", "h0", "h1", "w", "b", "d", "e")
+
+
+def tile(units):
+    return (16 * len(units), 128)
+
+
 TOK, ROWS, COLS, LIN = 160, 160, 1024, 80
 VMEM_LIMIT = 56_000_000
 
@@ -80,23 +86,21 @@
         src, dst = self.part.at[t, self._cut(h)], self.near.at[k, self._cut(h)]
         return t, put(src, dst, self.sems[2].at[k, h], self.sems[3].at[k, h], to)
 
-    def _add(self, t, got, h):
-        cut = self._cut(h)
-        self.part[t, cut] = self.part[t, cut] + got[cut]
-
-    def send_far(self, k, h):
-        t, copy = self._far(k, h)
+    def _send(self, make, slots, k):
+        copies = [make(k, h) for h in range(HALVES)]
+        t = copies[0][0]
         if k:
-            self._far(k - 1, h)[1].wait_recv()
-            self._add(t, self.far.at[k - 1], h)
-        copy.start()
-
-    def send_near(self, k, h):
-        t, copy = self._near(k, h)
-        if k:
-            self._near(k - 1, h)[1].wait_recv()
-            self._add(t, self.near.at[k - 1], h)
-        copy.start()
+            for h in range(HALVES):
+                make(k - 1, h)[1].wait_recv()
+            self.part[t] = self.part[t] + slots[k - 1]
+        for _, copy in copies:
+            copy.start()
+
+    def send_far(self, k):
+        self._send(self._far, self.far, k)
+
+    def send_near(self, k):
+        self._send(self._near, self.near, k)
 
     def finish(self):
         n = self.n // 2
@@ -109,7 +113,7 @@
         for h in range(HALVES):
             self._near(n - 2, h)[1].wait_recv()
             self._far(n - 1, h)[1].wait_recv()
-            loop((h + 1) * self.width, body, h * self.width)
+        loop(self.part.shape[1], body)
         return self.part.at[self.me]
 
     def drain(self):
@@ -163,24 +167,25 @@
     s["cz"], s["cy"] = pltpu.VMEM((7, 8, 128), F32), pltpu.VMEM((7, 8, 128), F32)
     for k, n in (("cx", 3), ("cz", 7), ("cy", 7)):
         s[k + "s"], s[k + "r"] = dma((n,)), dma((n,))
-    for u, order in enumerate(UNITS):
+    for p, (order, units) in enumerate(PARTS):
         n1, n2, n3 = (SIZE[k] for k in order)
-        s[f"u{u}"] = pltpu.VMEM((n1, n2, n3) + TILE, BF)
-        s[f"far{u}"] = pltpu.VMEM((n1 // 2, n2, n3) + TILE, BF)
-        s[f"near{u}"] = pltpu.VMEM((n1 // 2 - 1, n2, n3) + TILE, BF)
-        s[f"fs{u}"], s[f"fr{u}"] = dma((n1 // 2, HALVES)), dma((n1 // 2, HALVES))
-        s[f"ns{u}"], s[f"nr{u}"] = dma((n1 // 2 - 1, HALVES)), dma((n1 // 2 - 1, HALVES))
-        s[f"two{u}"] = pltpu.VMEM((n2 - 1, n3) + TILE, BF)
-        s[f"ts{u}"], s[f"tr{u}"] = dma((n2 - 1,)), dma((n2 - 1,))
-        s[f"v{u}"] = pltpu.VMEM((n3,) + TILE, BF)
-        s[f"three{u}"] = pltpu.VMEM((n3 - 1,) + TILE, BF)
-        s[f"hs{u}"], s[f"hr{u}"] = dma((n3 - 1,)), dma((n3 - 1,))
+        s[f"u{p}"] = pltpu.VMEM((n1, n2, n3) + tile(units), BF)
+        s[f"far{p}"] = pltpu.VMEM((n1 // 2, n2, n3) + tile(units), BF)
+        s[f"near{p}"] = pltpu.VMEM((n1 // 2 - 1, n2, n3) + tile(units), BF)
+        s[f"fs{p}"], s[f"fr{p}"] = dma((n1 // 2, HALVES)), dma((n1 // 2, HALVES))
+        s[f"ns{p}"], s[f"nr{p}"] = dma((n1 // 2 - 1, HALVES)), dma((n1 // 2 - 1, HALVES))
+        s[f"two{p}"] = pltpu.VMEM((n2 - 1, n3) + tile(units), BF)
+        s[f"ts{p}"], s[f"tr{p}"] = dma((n2 - 1,)), dma((n2 - 1,))
+    for k, (_, parts) in enumerate(LAST):
+        units = sum((PARTS[p][1] for p in parts), ())
+        s[f"v{k}"] = pltpu.VMEM((8,) + tile(units), BF)
+        s[f"three{k}"] = pltpu.VMEM((7,) + tile(units), BF)
+        s[f"hs{k}"], s[f"hr{k}"] = dma((7,)), dma((7,))
     s["base"] = pltpu.VMEM((16, LIN, 128), BF)
     s["basef"] = pltpu.VMEM((ROWS * 8, 128), F32)
     s["bs"], s["br"] = dma((8,)), dma((8,))
-    for w, units in enumerate(WAVES):
-        s[f"ag{w}"] = pltpu.VMEM((16, len(units)) + TILE, BF)
-        s[f"as{w}"], s[f"ar{w}"] = dma((15,)), dma((15,))
+    s["ag"] = pltpu.VMEM((16,) + tile(UNITS), BF)
+    s["as"], s["ar"] = dma((15,)), dma((15,))
     s["avg"] = pltpu.VMEM((ROWS * 8, 128), F32)
     return s
 
@@ -278,18 +283,20 @@
     base_z.start()
 
     rings = []
-    for u, order in enumerate(UNITS):
-        rings.append(Ring(here, sign, order[0], s[f"u{u}"], s[f"far{u}"], s[f"near{u}"],
-                          s[f"fs{u}"], s[f"fr{u}"], s[f"ns{u}"], s[f"nr{u}"]))
+    for p, (order, _) in enumerate(PARTS):
+        rings.append(Ring(here, sign, order[0], s[f"u{p}"], s[f"far{p}"], s[f"near{p}"],
+                          s[f"fs{p}"], s[f"fr{p}"], s[f"ns{p}"], s[f"nr{p}"]))
 
 
     def store(out, bz, bx, r0, t0, width):
-        for u, order in enumerate(UNITS):
-            for q in range(2):
-                for t in range(width):
-                    at = with_pq({"x": bx, "y": t0 + t, "z": bz * 2 + q, "c": c})
+        for p, (order, units) in enumerate(PARTS):
+            for i, u in enumerate(units):
+                for q in range(2):
                     r = r0 + u * 32 + q * 16
-                    s[f"u{u}"][at[order[0]], at[order[1]], at[order[2]]] = out[r:r + 16, t * 128:(t + 1) * 128]
+                    for t in range(width):
+                        at = with_pq({"x": bx, "y": t0 + t, "z": bz * 2 + q, "c": c})
+                        s[f"u{p}"][at[order[0]], at[order[1]], at[order[2]], i * 16:i * 16 + 16] = (
+                            out[r:r + 16, t * 128:(t + 1) * 128])
 
     def multiply(i):
         bx = (x + (2, -sign, sign, 0)[i] + 4) % 4
@@ -318,54 +325,57 @@
             acc -= weight * s["lp"][:, cols].astype(F32)
             store(acc.astype(BF), z // 2, x, 0, h * 2, 2)
 
-    def far(u, k, h=None):
-        for i in range(HALVES) if h is None else (h,):
-            rings[u].send_far(k, i)
-
-    def near(u, k, h=None):
-        for i in range(HALVES) if h is None else (h,):
-            rings[u].send_near(k, i)
-
-    def second(u):
-        part = rings[u].finish()
-        d = Direct(here, UNITS[u][1], part, s[f"two{u}"], s[f"ts{u}"], s[f"tr{u}"])
-        d.start()
-        twos[u] = d
-
-    def third(u):
-        d = twos[u]
-        d.arrive()
-
-        def body(i):
-            s[f"v{u}"][i] = d.total(i).astype(BF)
-
-        loop(SIZE[UNITS[u][2]], body)
-        e = Direct(here, UNITS[u][2], s[f"v{u}"], s[f"three{u}"], s[f"hs{u}"], s[f"hr{u}"])
-        e.start()
-        threes[u] = e
-
-    def wave_send(w, total):
-        for i, u in enumerate(WAVES[w]):
-            threes[u].arrive()
-            s[f"ag{w}"][g, i] = (total * threes[u].total()).astype(BF)
+    def far(u, k):
+        rings[u].send_far(k)
+
+    def near(u, k):
+        rings[u].send_near(k)
+
+    def second(p):
+        part = rings[p].finish()
+        twos[p] = Direct(here, PARTS[p][0][1], part, s[f"two{p}"], s[f"ts{p}"], s[f"tr{p}"])
+        twos[p].start()
+
+    def last(k):
+        axis, parts = LAST[k]
+        r = 0
+        for p in parts:
+            twos[p].arrive()
+            rows = 16 * len(PARTS[p][1])
+
+            def body(i, p=p, cut=slice(r, r + rows)):
+                s[f"v{k}"][i, cut] = twos[p].total(i).astype(BF)
+
+            loop(8, body)
+            r += rows
+        threes[k] = Direct(here, axis, s[f"v{k}"], s[f"three{k}"], s[f"hs{k}"], s[f"hr{k}"])
+        threes[k].start()
+
+    def ag_copy(j):
+        mine = s["ag"].at[g]
+        return put(mine, mine, s["as"].at[j - 1], s["ar"].at[j - 1], group_peer(j))
+
+    def ag_in(j):
+        theirs = s["ag"].at[(g - j + 16) % 16]
+        return put(theirs, theirs, s["as"].at[j - 1], s["ar"].at[j - 1], group_peer(j))
+
+    def averages():
+        r = 0
+        for k in range(len(LAST)):
+            threes[k].arrive()
+            rows = s[f"v{k}"].shape[1]
+            s["ag"][g, r:r + rows] = (known["scale"] * threes[k].total()).astype(BF)
+            r += rows
         for j in (8, 7, 9, 6, 10, 5, 11, 4, 12, 3, 13, 2, 14, 1, 15):
-            ag_copy(w, j).start()
-
-    def ag_copy(w, j):
-        mine = s[f"ag{w}"].at[g]
-        return put(mine, mine, s[f"as{w}"].at[j - 1], s[f"ar{w}"].at[j - 1], group_peer(j))
-
-    def ag_in(w, j):
-        theirs = s[f"ag{w}"].at[(g - j + 16) % 16]
-        return put(theirs, theirs, s[f"as{w}"].at[j - 1], s[f"ar{w}"].at[j - 1], group_peer(j))
-
-    def wave_end(w):
-        loop(16, lambda j: ag_in(w, j).wait_recv(), 1)
-        for i, u in enumerate(WAVES[w]):
+            ag_copy(j).start()
+
+    def new_rows():
+        loop(16, lambda j: ag_in(j).wait_recv(), 1)
+        for i, u in enumerate(UNITS):
             for yy in range(8):
                 for q in range(2):
                     r0 = u * 32 + q * 16
-                    avg = s[f"ag{w}"][yy * 2 + q, i].astype(F32)
+                    avg = s["ag"][yy * 2 + q, i * 16:i * 16 + 16].astype(F32)
                     s["avg"][pl.ds(r0 * 8 + yy, 16, stride=8), :] = avg
                     base = s["basef"][pl.ds(r0 * 8 + yy, 16, stride=8), :]
                     np_ref[r0:r0 + 16, yy * 128:(yy + 1) * 128] = (base + 1.33 * avg).astype(BF)
@@ -418,8 +428,7 @@
         "m": multiply, "q": base_step,
         "x": counts_x, "t": counts, "c": total_count, "b": base_rows, "d": drain,
         "o": lambda: multiply_own(2.0 * known["count"][0:1, 0:1]),
-        "f": far, "n": near, "s": second, "h": third,
-        "w": lambda w: wave_send(w, known["scale"]), "e": wave_end,
+        "f": far, "n": near, "s": second, "h": last, "w": averages, "e": new_rows,
     }
     for step in PLAN:
         steps[step[0]](*(int(v) for v in step[1:]))
@@ -430,8 +439,7 @@
     moment = 0.9 * mom_ref[...] + delta
     nm_ref[...] = moment
     na_ref[...] = anc - 0.7 * (delta + 0.9 * moment)
-    for w in range(len(WAVES)):
-        loop(16, lambda j, w=w: ag_copy(w, j).wait_send(), 1)
+    loop(16, lambda j: ag_copy(j).wait_send(), 1)
 
 
 def local(activations, cotangent, live, local_params, anchor, momentum):

time: 73.1 us -> 71.9 us (0.984)
  Pallas kernels: 68 us -> 66.8 us
    pallas_call x1, Pallas kernels: 68 us -> 66.8 us  [local(): pl.pallas_call(kernel, name='outer_step', out_shape=(jax.ShapeDtypeStruct...]
where the time goes in v3:
time: 71.9 us; the launch traced here: 71.6 us
  Pallas kernels  66.8 us (93%)
  local copies, waits for them, and re-layouts  3.51 us (5%)
  between operations  1.3 us (2%)
    pallas_call x1, Pallas kernels, local(): pl.pallas_call(kernel, name='outer_step', out_shape=(jax.ShapeDtypeStruct...  66.8 us
    unnamed x7, local copies, waits for them, and re-layouts  3.51 us

profile of v3, /device:TPU:8, one launch (start us, length us, event | category | flops | bytes accessed | tf_op | source)
XLA Modules:
  0.0 71.6 jit_solution(1126222145225016507)
XLA Ops:
  1.3 0.0 copy-start
  1.3 0.8 %copy-done = f32[1,10,1024]{2,0,1:T(1,128)S(1)} copy-done((f32[1,10,1024]{2,0,1:T(1,128)S(1)}, f32[1,10,1024]{2,0,1:T(1,128)}, u32[]{:S(2)}) %copy-start) | copy-done | bytes 40984
  2.1 0.0 copy-start.1
  2.1 0.8 %copy-done.1 = f32[1,10,1024]{2,0,1:T(1,128)S(1)} copy-done((f32[1,10,1024]{2,0,1:T(1,128)S(1)}, f32[1,10,1024]{2,0,1:T(1,128)}, u32[]{:S(2)}) %copy-start.1) | copy-done | bytes 40984
  2.8 66.8 %outer_step.1 = (bf16[160,1024]{1,0:T(8,128)(2,1)S(1)}, f32[80,128]{1,0:T(8,128)S(1)}, f32[80,128]{1,0:T(8,128)S(1)}) custom-call(s32[1,1]{1,0:T(1,128)S(6)} %copy.16.live_hbm, bf16[160,5120]{1,0:T(8,128)(2,1)} %bitcast.11, bf16[160,1024]{1,0:T(8,128)(2,1)} %bitcast.12, bf16[160,1024]{1,0:T(8,128)(2,1)} %bitcast.13, f32[80,128]{1,0:T(8,128)S(1)} %bitcast.9, ...), custom_call_target="tpu_custom_call" | custom-call | tf_op jit(solution)/shard_map/outer_step/pallas_call | solution.py:448
  69.6 0.7 %copy.17 = bf16[160,1024]{1,0:T(8,128)(2,1)} copy(bf16[160,1024]{1,0:T(8,128)(2,1)S(1)} %get-tuple-element.18) | data formatting | bytes 655360
  70.4 0.6 copy.18
  71.0 0.6 copy.19
Async XLA Ops:
  1.3 0.8 %copy-start = (f32[1,10,1024]{2,0,1:T(1,128)S(1)}, f32[1,10,1024]{2,0,1:T(1,128)}, u32[]{:S(2)}) copy-start(f32[1,10,1024]{2,0,1:T(1,128)} %param.10) | copy-start | bytes 122884
  2.1 0.8 %copy-start.1 = (f32[1,10,1024]{2,0,1:T(1,128)S(1)}, f32[1,10,1024]{2,0,1:T(1,128)}, u32[]{:S(2)}) copy-start(f32[1,10,1024]{2,0,1:T(1,128)} %param.11) | copy-start | bytes 122884

commit v4 on v3

--- a/solution.py
+++ b/solution.py
@@ -253,7 +253,7 @@
     ex = [put(s["cv"].at[0], s["cc"], s["exs"].at[0], s["exr"].at[0], partner),
           put(s["m"], s["mp"], s["exs"].at[1], s["exr"].at[1], partner)]
     ex += [ex_copy(i, (x + dx + 4) % 4) for i, dx in enumerate((2, sign, -sign, 0))]
-    for copy in ex[:4]:
+    for copy in ex:
         copy.start()
 
     zpartner = device({**here, "z": z + 1 - 2 * zl})
@@ -304,8 +304,6 @@
         if i == 0:
             ex[1].wait_recv()
         ex_copy(i, bx).wait_recv()
-        if i < 2:
-            ex[4 + i].start()
         mine = s["at"][c, :, rows, :].reshape(4 * ROWS, TOK)
         theirs = s["atp"][:, rows, :].reshape(4 * ROWS, TOK)
         for h in range(4):

time: 71.9 us -> 71.9 us (level)
  no operation moved by 1% of the time
where the time goes in v4:
time: 71.9 us; the launch traced here: 71.6 us
  Pallas kernels  66.8 us (93%)
  local copies, waits for them, and re-layouts  3.51 us (5%)
  between operations  1.3 us (2%)
    pallas_call x1, Pallas kernels, local(): pl.pallas_call(kernel, name='outer_step', out_shape=(jax.ShapeDtypeStruct...  66.8 us
    unnamed x7, local copies, waits for them, and re-layouts  3.51 us

profile of v4, /device:TPU:8, one launch (start us, length us, event | category | flops | bytes accessed | tf_op | source)
XLA Modules:
  0.0 71.6 jit_solution(4853970309277493134)
XLA Ops:
  1.3 0.0 copy-start
  1.3 0.8 %copy-done = f32[1,10,1024]{2,0,1:T(1,128)S(1)} copy-done((f32[1,10,1024]{2,0,1:T(1,128)S(1)}, f32[1,10,1024]{2,0,1:T(1,128)}, u32[]{:S(2)}) %copy-start) | copy-done | bytes 40984
  2.1 0.0 copy-start.1
  2.1 0.8 %copy-done.1 = f32[1,10,1024]{2,0,1:T(1,128)S(1)} copy-done((f32[1,10,1024]{2,0,1:T(1,128)S(1)}, f32[1,10,1024]{2,0,1:T(1,128)}, u32[]{:S(2)}) %copy-start.1) | copy-done | bytes 40984
  2.8 66.8 %outer_step.1 = (bf16[160,1024]{1,0:T(8,128)(2,1)S(1)}, f32[80,128]{1,0:T(8,128)S(1)}, f32[80,128]{1,0:T(8,128)S(1)}) custom-call(s32[1,1]{1,0:T(1,128)S(6)} %copy.16.live_hbm, bf16[160,5120]{1,0:T(8,128)(2,1)} %bitcast.11, bf16[160,1024]{1,0:T(8,128)(2,1)} %bitcast.12, bf16[160,1024]{1,0:T(8,128)(2,1)} %bitcast.13, f32[80,128]{1,0:T(8,128)S(1)} %bitcast.9, ...), custom_call_target="tpu_custom_call" | custom-call | tf_op jit(solution)/shard_map/outer_step/pallas_call | solution.py:446
  69.7 0.7 %copy.17 = bf16[160,1024]{1,0:T(8,128)(2,1)} copy(bf16[160,1024]{1,0:T(8,128)(2,1)S(1)} %get-tuple-element.18) | data formatting | bytes 655360
  70.4 0.6 copy.18
  71.0 0.6 copy.19
Async XLA Ops:
  1.3 0.8 %copy-start = (f32[1,10,1024]{2,0,1:T(1,128)S(1)}, f32[1,10,1024]{2,0,1:T(1,128)}, u32[]{:S(2)}) copy-start(f32[1,10,1024]{2,0,1:T(1,128)} %param.10) | copy-start | bytes 122884
  2.1 0.8 %copy-start.1 = (f32[1,10,1024]{2,0,1:T(1,128)S(1)}, f32[1,10,1024]{2,0,1:T(1,128)}, u32[]{:S(2)}) copy-start(f32[1,10,1024]{2,0,1:T(1,128)} %param.11) | copy-start | bytes 122884
